TPU v7x, 512 devices: a whole 4x8x8 slice. The times are simulated.
512 devices in a mesh: label: 64 (over y, x, core), query: 8 (over z).
Axes of the slice: x: 4, y: 8, z: 8, core: 2. Of those that a mesh axis runs over, the one named last changes fastest.
Arguments:
- queries: bfloat16 [1536, 768], P('query'), may hold values from -6 to 6
- label_ids: int32 [1536, 10], P('query'), may hold values from 0 to 4095, as said below
- label_text: bfloat16 [4096, 32, 768], P('label'), may hold values from -16 to 16
- up_weight: bfloat16 [768, 3072], P(None, 'query'), may hold values from -0.21875 to 0.21875
- down_weight: bfloat16 [768, 3072], P(None, 'query'), may hold values from -0.109375 to 0.109375
- free_vectors: float32 [4096, 768], P('label'), may hold values from -4 to 4
- moments: float32 [4096, 768], P('label'), may hold values from -0.06 to 0.06
- seconds: float32 [4096, 768], P('label'), may hold values from 1e-05 to 0.001
Outputs:
- free_new: float32 [4096, 768], P('label')
- moments_new: float32 [4096, 768], P('label')
- seconds_new: float32 [4096, 768], P('label')
- query_grad: float32 [1536, 768], P('query')
- up_grad: float32 [768, 3072], P('label', 'query')
- down_grad: float32 [768, 3072], P('label', 'query')
Inputs may be any that keep to these rules, and one draw needn't show every extreme that they name: `label_ids`: the 10 ids of one query are distinct.
All inputs are finite; a program needn't handle non-finite values.
Results may differ from a plain program's by a relative error of at most 0.023.
Values sent between devices are 32-bit elements; how exact they have to be, the bound alone decides.
A program may use at most 64 MiB of HBM per device.

v0:
```python
import jax
import jax.numpy as jnp
from jax import lax
from jax.sharding import PartitionSpec as P

beta_one = 0.9
beta_two = 0.999
adam_eps = 1e-08
learn_rate = 0.05
first_fix = 1.0 - 0.9**10
second_fix = 1.0 - 0.999**10


def gelu_tanh(values):
    return jax.nn.gelu(values, approximate=True)


def body(queries, label_ids, label_text, up_weight, down_weight, free_vectors, moments, seconds):
    label_rows, text_len, model_width = label_text.shape
    unit_cols = up_weight.shape[1]
    temper = 1.0 / jnp.sqrt(jnp.float32(model_width))
    text_rows = label_text.reshape(label_rows * text_len, model_width)
    preact = jnp.dot(text_rows, up_weight, preferred_element_type=jnp.float32)
    hidden = gelu_tanh(preact).astype(jnp.bfloat16)
    pooled_hidden = jnp.mean(
        hidden.reshape(label_rows, text_len, unit_cols), axis=1, dtype=jnp.float32
    )
    pooled_text = jnp.mean(label_text, axis=1, dtype=jnp.float32)
    encoded_part = jnp.einsum(
        "lf,df->ld", pooled_hidden, down_weight.astype(jnp.float32), precision=lax.Precision.HIGHEST
    )
    encoded = lax.psum(encoded_part, "query")
    label_vec = pooled_text + encoded + free_vectors
    label_bf = label_vec.astype(jnp.bfloat16)
    first_label = lax.axis_index("label") * label_rows
    local_ids = label_ids - first_label
    owners = (
        local_ids[:, :, None] == jnp.arange(label_rows, dtype=jnp.int32)[None, None, :]
    ).astype(jnp.float32)
    similar = jnp.einsum("id,jd->ij", queries, label_bf, preferred_element_type=jnp.float32)
    partial_value = jnp.einsum("ikj,ij->ik", owners, similar, precision=lax.Precision.HIGHEST)
    scores = lax.psum(partial_value, "label") * temper
    likely = jax.nn.softmax(scores, axis=-1)
    target = jnp.where(jnp.arange(scores.shape[1]) < 2, 0.5, 0.0).astype(jnp.float32)
    pair_coef = ((likely - target[None, :]) * temper).astype(jnp.bfloat16)
    spread = jnp.einsum(
        "ik,ikj->ij", pair_coef.astype(jnp.float32), owners, precision=lax.Precision.HIGHEST
    ).astype(jnp.bfloat16)
    query_terms = jnp.dot(spread, label_bf, preferred_element_type=jnp.float32)
    query_grad = lax.psum(query_terms, "label")
    grad_part = jnp.einsum("ij,id->jd", spread, queries, preferred_element_type=jnp.float32)
    count_part = jnp.sum(owners, axis=(0, 1))
    label_grad, counts = lax.psum((grad_part, count_part), "query")
    out_grad = label_grad.astype(jnp.bfloat16)
    hidden_grad = jnp.dot(out_grad, down_weight, preferred_element_type=jnp.float32) / text_len
    token_grad = jnp.broadcast_to(
        hidden_grad[:, None, :], (label_rows, text_len, unit_cols)
    ).reshape(label_rows * text_len, unit_cols)
    preact_grad = jax.vjp(gelu_tanh, preact)[1](token_grad)[0].astype(jnp.bfloat16)
    joined = lax.psum_scatter(
        jnp.concatenate(
            (
                lax.dot_general(
                    text_rows,
                    preact_grad,
                    (((0,), (0,)), ((), ())),
                    preferred_element_type=jnp.float32,
                ),
                jnp.einsum(
                    "ld,lf->df",
                    out_grad.astype(jnp.float32),
                    pooled_hidden,
                    precision=lax.Precision.HIGHEST,
                ),
            ),
            axis=1,
        ),
        "label",
        scatter_dimension=0,
        tiled=True,
    )
    up_part = joined[:, :unit_cols]
    down_part = joined[:, unit_cols:]
    touched = (counts > 0.5)[:, None]
    moment_step = beta_one * moments + (1.0 - beta_one) * label_grad
    second_step = beta_two * seconds + (1.0 - beta_two) * label_grad * label_grad
    update = (
        learn_rate * (moment_step / first_fix) / (jnp.sqrt(second_step / second_fix) + adam_eps)
    )
    free_new = jnp.where(touched, free_vectors - update, free_vectors)
    moments_new = jnp.where(touched, moment_step, moments)
    seconds_new = jnp.where(touched, second_step, seconds)
    return (free_new, moments_new, seconds_new, query_grad, up_part, down_part)


def solution(mesh):
    placed = (
        P("query", None),
        P("query", None),
        P("label", None, None),
        P(None, "query"),
        P(None, "query"),
        P("label", None),
        P("label", None),
        P("label", None),
    )
    return jax.shard_map(
        body,
        mesh=mesh,
        in_specs=placed,
        out_specs=(
            P("label", None),
            P("label", None),
            P("label", None),
            P("query", None),
            P("label", "query"),
            P("label", "query"),
        ),
        check_vma=False,
    )
```

profile of v0, /device:TPU:25, one launch (start us, length us, event | category | flops | bytes accessed | tf_op | source)
XLA Modules:
  0.0 643.8 jit_solution(12416014666471665310)
XLA Ops:
  7.2 0.0 copy-start
  7.2 0.0 all-reduce.6.cloned.1.call-start
  7.2 1.0 copy-done
  8.2 0.0 copy-start.2
  8.2 6.1 convert_reduce_fusion.1
  14.4 0.0 copy-start.8
  14.4 0.0 copy-start.5
  14.4 0.0 copy-start.4
  14.4 0.0 copy-done.2
  14.4 1.3 fusion.16
  15.7 0.0 all-reduce.6.cloned.1.call-update
  15.7 0.0 all-reduce.8.cloned.1.call-start
  15.8 2.9 convert_reduce_fusion
  18.7 0.0 copy-done.8
  18.7 75.3 %all-reduce.6.cloned.1.call-done = f32[64,768]{1,0:T(8,128)} async-done(((f32[64,768]{1,0:T(8,128)}), f32[64,768]{1,0:T(8,128)}) %all-reduce.6.cloned.1.call-update) | async-done | bytes 196624 | tf_op jit(solution)/shard_map/psum | solution.py:32
  94.0 0.0 copy-done.5
  94.0 1.0 add_convert_fusion
  95.0 0.0 copy-done.4
  95.0 0.2 convolution_bitcast_fusion.1
  95.2 0.1 select_reduce_fusion.1
  95.3 235.5 %psum.37 = f32[192,10]{0,1:T(8,128)S(1)} all-reduce(f32[192,10]{0,1:T(8,128)S(1)} %select_reduce_fusion.1), channel_id=1, replica_groups=mesh['label'=64,'query'=8] {'label'}, use_global_device_ids=true, to_apply=%region_5.0 | all-reduce | flops 1920 | bytes 15360 | tf_op jit(solution)/shard_map/psum | solution.py:42
  330.9 0.1 fusion.27
  330.9 0.2 convert_reduce_fusion.2
  331.2 0.1 copy.31
  331.3 0.9 fusion.32
  332.2 0.0 all-reduce.8.cloned.1.call-update
  332.2 0.0 all-reduce.10.cloned.1.call-start
  332.3 1.0 fusion.31
  333.3 83.8 %all-reduce.8.cloned.1.call-done = f32[64,768]{1,0:T(8,128)} async-done(((f32[64,768]{1,0:T(8,128)}), f32[64,768]{1,0:T(8,128)}) %all-reduce.8.cloned.1.call-update) | async-done | bytes 196624 | tf_op jit(solution)/shard_map/psum | solution.py:53
  417.1 0.0 copy-start.1
  417.1 1.3 convolution_multiply_fusion
  418.4 3.6 fusion.6
  422.0 0.0 copy-done.1
  422.0 0.0 copy-start.3
  422.0 1.4 convolution_bitcast_fusion
  423.5 0.0 copy-done.3
  423.5 0.7 fusion.14
  424.2 0.0 copy-start.6
  424.2 0.0 copy-start.7
  424.2 1.5 pad_maximum_fusion
  425.7 0.0 all-reduce.10.cloned.1.call-update
  425.7 1.3 dynamic-slice
  427.7 12.6 %psum.35 = f32[64]{0:T(128)S(1)} all-reduce(f32[64]{0:T(128)S(1)} %get-tuple-element.24), channel_id=1, replica_groups=mesh['label'=64,'query'=8] {'query'}, use_global_device_ids=true, to_apply=%region_1.0 | all-reduce | flops 64 | bytes 512 | tf_op jit(solution)/shard_map/psum | solution.py:53
  440.3 0.0 copy-done.6
  440.3 0.0 copy-done.7
  440.3 1.0 fusion.13
  441.3 191.3 %all-reduce.10.cloned.1.call-done = (f32[192,768]{1,0:T(8,128)}, f32[768,768]{0,1:T(8,128)}) async-done(((f32[192,768]{1,0:T(8,128)}, f32[768,768]{0,1:T(8,128)}), (f32[192,768]{1,0:T(8,128)}, f32[768,768]{0,1:T(8,128)})) %all-reduce.10.cloned.1.call-update) | async-done | bytes 2949136 | tf_op jit(solution)/shard_map/psum | solution.py:50
  632.7 1.3 fusion.30
  633.9 0.7 copy.20
  634.7 0.7 copy.21
  635.4 1.9 copy.41
  (5 shorter events, 0.1 us)
Async XLA Ops:
  7.2 1.1 copy-start
  7.2 86.8 %all-reduce.6.cloned.1.call-start = ((), (), s32[]{:S(2)}) async-start(), calls=%async_computation | async-start | bytes 393216 | tf_op jit(solution)/shard_map/psum | solution.py:32
  8.2 6.1 copy-start.2
  14.4 4.3 copy-start.8
  14.4 79.7 %copy-start.5 = (f32[64,768]{1,0:T(8,128)S(1)}, f32[64,768]{1,0:T(8,128)}, u32[]{:S(2)}) copy-start(f32[64,768]{1,0:T(8,128)} %param.13) | copy-start | bytes 589828
  14.4 80.6 %copy-start.4 = (bf16[192,768]{1,0:T(8,128)(2,1)S(1)}, bf16[192,768]{1,0:T(8,128)(2,1)}, u32[]{:S(2)}) copy-start(bf16[192,768]{1,0:T(8,128)(2,1)} %param.8) | copy-start | bytes 884740
  15.7 401.4 %all-reduce.8.cloned.1.call-start = ((), (), s32[]{:S(2)}) async-start(), calls=%async_computation.1 | async-start | bytes 393216 | tf_op jit(solution)/shard_map/psum | solution.py:53
  332.2 300.4 %all-reduce.10.cloned.1.call-start = ((), (), s32[]{:S(2)}) async-start(), calls=%async_computation.2 | async-start | bytes 5898240 | tf_op jit(solution)/shard_map/psum | solution.py:50
  417.1 4.9 copy-start.1
  422.0 1.5 copy-start.3
  424.2 16.2 %copy-start.6 = (f32[64,768]{1,0:T(8,128)S(1)}, f32[64,768]{1,0:T(8,128)}, u32[]{:S(2)}) copy-start(f32[64,768]{1,0:T(8,128)} %param.15) | copy-start | bytes 589828
  424.2 16.2 %copy-start.7 = (f32[64,768]{1,0:T(8,128)S(1)}, f32[64,768]{1,0:T(8,128)}, u32[]{:S(2)}) copy-start(f32[64,768]{1,0:T(8,128)} %param.14) | copy-start | bytes 589828
Sparse Core Ops, SparseCore 0:
  15.8 78.1 all-reduce.5
  332.3 84.7 all-reduce.7
  425.9 206.7 all-reduce.9
where the time goes:
time: 644 us
  waiting for transfers between devices  351 us (55%)
  blocking collectives  248 us (39%)
  between operations  14.6 us (2%)
  matrix products  13 us (2%)
  other arithmetic  10.4 us (2%)
  local copies, waits for them, and re-layouts  7.07 us (1%)
    psum x1, blocking collectives, body(): scores = lax.psum(partial_value, 'label') * temper  235 us
    psum x1, waiting for transfers between devices, body(): query_grad = lax.psum(query_terms, 'label')  191 us
    psum x1, waiting for transfers between devices, body(): label_grad, counts = lax.psum((grad_part, count_part), 'query')  83.8 us
    psum x1, waiting for transfers between devices, body(): encoded = lax.psum(encoded_part, 'query')  75.3 us
  transfers between devices with their start and end apart: 3, of which 3 were waited for; matrix products, arithmetic and copies ran while one was open for 1% of the time, Pallas kernels for 0%

commit v1 on v0

--- a/solution.py
+++ b/solution.py
@@ -9,6 +9,15 @@
 learn_rate = 0.05
 first_fix = 1.0 - 0.9**10
 second_fix = 1.0 - 0.999**10
+
+
+def added_up(x, axis):
+    size = lax.axis_size(axis)
+    acc, far = (x, 1)
+    while far < size:
+        acc = acc + lax.ppermute(acc, axis, [(i, i ^ far) for i in range(size)])
+        far = 2 * far
+    return acc
 
 
 def gelu_tanh(values):
@@ -29,7 +38,7 @@
     encoded_part = jnp.einsum(
         "lf,df->ld", pooled_hidden, down_weight.astype(jnp.float32), precision=lax.Precision.HIGHEST
     )
-    encoded = lax.psum(encoded_part, "query")
+    encoded = added_up(encoded_part, "query")
     label_vec = pooled_text + encoded + free_vectors
     label_bf = label_vec.astype(jnp.bfloat16)
     first_label = lax.axis_index("label") * label_rows

time: 644 us -> 603 us (0.936)
  waiting for transfers between devices: 351 us -> 295 us
  starting transfers between devices: 0.12 us -> 17.9 us
    psum x1 -> x0, waiting for transfers between devices: 75.3 us -> none  [body(): encoded = lax.psum(encoded_part, 'query')]
    ppermute x0 -> x3, starting transfers between devices: none -> 17.8 us  [added_up(): acc = acc + lax.ppermute(acc, axis, [(i, i ^ far) for i in range(size)])]
    ppermute x0 -> x3, waiting for transfers between devices: none -> 17 us  [added_up(): acc = acc + lax.ppermute(acc, axis, [(i, i ^ far) for i in range(size)])]
  transfers between devices with their start and end apart: 3 -> 5, of which waited for: 3 -> 5; matrix products, arithmetic and copies ran while one was open for 1% -> 1% of each run, Pallas kernels for 0% -> 0%
where the time goes in v1:
time: 603 us; the launch traced here: 602 us
  waiting for transfers between devices  295 us (49%)
  blocking collectives  246 us (41%)
  starting transfers between devices  17.9 us (3%)
  between operations  14.9 us (2%)
  matrix products  12.3 us (2%)
  other arithmetic  9.56 us (2%)
  local copies, waits for them, and re-layouts  7.07 us (1%)
    psum x1, blocking collectives, body(): scores = lax.psum(partial_value, 'label') * temper  233 us
    psum x1, waiting for transfers between devices, body(): query_grad = lax.psum(query_terms, 'label')  191 us
    psum x1, waiting for transfers between devices, body(): label_grad, counts = lax.psum((grad_part, count_part), 'query')  86.7 us
    ppermute x3, starting transfers between devices, added_up(): acc = acc + lax.ppermute(acc, axis, [(i, i ^ far) for i in range(size)])  17.8 us
    ppermute x3, waiting for transfers between devices, added_up(): acc = acc + lax.ppermute(acc, axis, [(i, i ^ far) for i in range(size)])  17 us
    psum x1, blocking collectives, body(): label_grad, counts = lax.psum((grad_part, count_part), 'query')  12.6 us
  transfers between devices with their start and end apart: 5, of which 5 were waited for; matrix products, arithmetic and copies ran while one was open for 1% of the time, Pallas kernels for 0%

profile of v1, /device:TPU:25, one launch (start us, length us, event | category | flops | bytes accessed | tf_op | source)
XLA Modules:
  0.0 602.1 jit_solution(14149343054252642478)
XLA Ops:
  7.2 0.0 copy-start
  7.2 0.0 all-reduce.5.cloned.1.call-start
  7.2 1.0 copy-done
  8.2 0.0 copy-start.2
  8.2 6.1 %convert_reduce_fusion.1 = (f32[64,384]{1,0:T(8,128)S(1)}, f32[2048,384]{1,0:T(8,128)}) fusion(bf16[2048,768]{1,0:T(8,128)(2,1)} %bitcast.40, bf16[768,384]{1,0:T(8,128)(2,1)S(1)} %copy-done), kind=kOutput, calls=%fused_computation.15 | convolution fusion | flops 1216585728 | bytes 6979584 | tf_op jit(solution)/shard_map/dot_general | solution.py:32
  14.4 0.0 copy-start.8
  14.4 0.0 copy-start.5
  14.4 0.0 copy-done.2
  14.4 0.0 copy-start.4
  14.4 0.6 fusion.16
  15.0 4.0 collective-permute-start
  19.0 4.6 collective-permute-done
  23.7 5.8 collective-permute-start.1
  29.5 2.9 convert_reduce_fusion
  32.4 5.8 collective-permute-done.1
  38.2 8.0 %collective-permute-start.2 = (f32[64,768]{1,0:T(8,128)S(1)}, f32[64,768]{1,0:T(8,128)S(1)}, u32[]{:S(2)}, u32[]{:S(2)}) collective-permute-start(f32[64,768]{1,0:T(8,128)S(1)} %add.49), channel_id=1, source_target_pairs={{0,4},{1,5},{2,6},{3,7},{4,0},{5,1},{6,2},{7,3},{8,12},{9,13},{10,... | collective-permute-start | bytes 589832 | tf_op jit(solution)/shard_map/ppermute | solution.py:18
  46.2 0.0 copy-done.8
  46.2 6.6 %collective-permute-done.2 = f32[64,768]{1,0:T(8,128)S(1)} collective-permute-done((f32[64,768]{1,0:T(8,128)S(1)}, f32[64,768]{1,0:T(8,128)S(1)}, u32[]{:S(2)}, u32[]{:S(2)}) %collective-permute-start.2) | collective-permute-done | bytes 196640 | tf_op jit(solution)/shard_map/ppermute | solution.py:18
  52.8 0.0 copy-done.5
  52.8 0.1 add_convert_fusion
  52.9 0.0 copy-done.4
  52.9 0.2 convolution_bitcast_fusion.1
  53.1 0.1 select_reduce_fusion.1
  53.2 233.1 %psum.29 = f32[192,10]{0,1:T(8,128)S(1)} all-reduce(f32[192,10]{0,1:T(8,128)S(1)} %select_reduce_fusion.1), channel_id=1, replica_groups=mesh['label'=64,'query'=8] {'label'}, use_global_device_ids=true, to_apply=%region_4.0 | all-reduce | flops 1920 | bytes 15360 | tf_op jit(solution)/shard_map/psum | solution.py:51
  286.4 0.1 fusion.27
  286.5 0.2 convert_reduce_fusion.2
  286.7 0.1 copy.31
  286.8 0.9 fusion.32
  287.7 0.0 all-reduce.5.cloned.1.call-update
  287.7 0.0 all-reduce.7.cloned.1.call-start
  287.8 1.0 fusion.31
  288.8 86.7 %all-reduce.5.cloned.1.call-done = f32[64,768]{1,0:T(8,128)} async-done(((f32[64,768]{1,0:T(8,128)}), f32[64,768]{1,0:T(8,128)}) %all-reduce.5.cloned.1.call-update) | async-done | bytes 196624 | tf_op jit(solution)/shard_map/psum | solution.py:62
  375.5 0.0 copy-start.1
  375.5 1.3 convolution_multiply_fusion
  376.8 3.6 fusion.6
  380.4 0.0 copy-done.1
  380.4 0.0 copy-start.3
  380.4 1.4 convolution_bitcast_fusion
  381.8 0.0 copy-done.3
  381.9 0.7 fusion.14
  382.5 0.0 copy-start.6
  382.5 0.0 copy-start.7
  382.6 1.5 pad_maximum_fusion
  384.1 0.0 all-reduce.7.cloned.1.call-update
  384.1 1.3 dynamic-slice
  386.0 12.6 %psum.28 = f32[64]{0:T(128)S(1)} all-reduce(f32[64]{0:T(128)S(1)} %get-tuple-element.24), channel_id=1, replica_groups=mesh['label'=64,'query'=8] {'query'}, use_global_device_ids=true, to_apply=%region_1.0 | all-reduce | flops 64 | bytes 512 | tf_op jit(solution)/shard_map/psum | solution.py:62
  398.7 0.0 copy-done.6
  398.7 0.0 copy-done.7
  398.7 1.0 fusion.13
  399.7 190.9 %all-reduce.7.cloned.1.call-done = (f32[192,768]{1,0:T(8,128)}, f32[768,768]{0,1:T(8,128)}) async-done(((f32[192,768]{1,0:T(8,128)}, f32[768,768]{0,1:T(8,128)}), (f32[192,768]{1,0:T(8,128)}, f32[768,768]{0,1:T(8,128)})) %all-reduce.7.cloned.1.call-update) | async-done | bytes 2949136 | tf_op jit(solution)/shard_map/psum | solution.py:59
  590.6 1.3 fusion.30
  591.9 0.7 copy.20
  592.6 0.7 copy.21
  593.4 1.9 copy.40
  (7 shorter events, 0.1 us)
Async XLA Ops:
  7.2 1.1 copy-start
  7.2 368.3 %all-reduce.5.cloned.1.call-start = ((), (), s32[]{:S(2)}) async-start(), calls=%async_computation | async-start | bytes 393216 | tf_op jit(solution)/shard_map/psum | solution.py:62
  8.2 6.1 %copy-start.2 = (bf16[768,384]{1,0:T(8,128)(2,1)S(1)}, bf16[768,384]{1,0:T(8,128)(2,1)}, u32[]{:S(2)}) copy-start(bf16[768,384]{1,0:T(8,128)(2,1)} %param.12) | copy-start | bytes 1769476
  14.4 31.8 %copy-start.8 = (s32[192,10]{0,1:T(8,128)S(1)}, s32[192,10]{0,1:T(8,128)}, u32[]{:S(2)}) copy-start(s32[192,10]{0,1:T(8,128)} %param.9) | copy-start | bytes 23044
  14.4 38.5 %copy-start.5 = (f32[64,768]{1,0:T(8,128)S(1)}, f32[64,768]{1,0:T(8,128)}, u32[]{:S(2)}) copy-start(f32[64,768]{1,0:T(8,128)} %param.13) | copy-start | bytes 589828
  14.4 38.5 %copy-start.4 = (bf16[192,768]{1,0:T(8,128)(2,1)S(1)}, bf16[192,768]{1,0:T(8,128)(2,1)}, u32[]{:S(2)}) copy-start(bf16[192,768]{1,0:T(8,128)(2,1)} %param.8) | copy-start | bytes 884740
  15.0 8.6 %collective-permute-start = (f32[64,768]{1,0:T(8,128)S(1)}, f32[64,768]{1,0:T(8,128)S(1)}, u32[]{:S(2)}, u32[]{:S(2)}) collective-permute-start(f32[64,768]{1,0:T(8,128)S(1)} %fusion.16), channel_id=1, source_target_pairs={{0,1},{1,0},{2,3},{3,2},{4,5},{5,4},{6,7},{7,6},{8,9},{9,8},{10,11... | collective-permute-start | bytes 589832 | tf_op jit(solution)/shard_map/ppermute | solution.py:18
  23.7 14.5 %collective-permute-start.1 = (f32[64,768]{1,0:T(8,128)S(1)}, f32[64,768]{1,0:T(8,128)S(1)}, u32[]{:S(2)}, u32[]{:S(2)}) collective-permute-start(f32[64,768]{1,0:T(8,128)S(1)} %add.48), channel_id=1, source_target_pairs={{0,2},{1,3},{2,0},{3,1},{4,6},{5,7},{6,4},{7,5},{8,10},{9,11},{10,... | collective-permute-start | bytes 589832 | tf_op jit(solution)/shard_map/ppermute | solution.py:18
  38.2 14.7 %collective-permute-start.2 = (f32[64,768]{1,0:T(8,128)S(1)}, f32[64,768]{1,0:T(8,128)S(1)}, u32[]{:S(2)}, u32[]{:S(2)}) collective-permute-start(f32[64,768]{1,0:T(8,128)S(1)} %add.49), channel_id=1, source_target_pairs={{0,4},{1,5},{2,6},{3,7},{4,0},{5,1},{6,2},{7,3},{8,12},{9,13},{10,... | collective-permute-start | bytes 589832 | tf_op jit(solution)/shard_map/ppermute | solution.py:18
  287.7 302.9 %all-reduce.7.cloned.1.call-start = ((), (), s32[]{:S(2)}) async-start(), calls=%async_computation.1 | async-start | bytes 5898240 | tf_op jit(solution)/shard_map/psum | solution.py:59
  375.5 4.9 copy-start.1
  380.4 1.4 copy-start.3
  382.5 16.2 %copy-start.6 = (f32[64,768]{1,0:T(8,128)S(1)}, f32[64,768]{1,0:T(8,128)}, u32[]{:S(2)}) copy-start(f32[64,768]{1,0:T(8,128)} %param.15) | copy-start | bytes 589828
  382.5 16.2 %copy-start.7 = (f32[64,768]{1,0:T(8,128)S(1)}, f32[64,768]{1,0:T(8,128)}, u32[]{:S(2)}) copy-start(f32[64,768]{1,0:T(8,128)} %param.14) | copy-start | bytes 589828
Sparse Core Ops, SparseCore 0:
  287.8 87.6 all-reduce.4
  384.2 206.3 all-reduce.6
